TPU v7x, 32 devices: a whole 2x2x4 slice. The times are simulated.
32 devices in a mesh: row: 8 (over z, x), col: 4 (over y, core).
Axes of the slice: x: 2, y: 2, z: 4, core: 2. Of those that a mesh axis runs over, the one named last changes fastest.
Arguments:
- vectors: float32 [65536, 2048], P('row', 'col'), may hold values from -6 to 6
- reflectors: float32 [65536, 256], P('row'), may hold values from -0.09375 to 0.09375
- panel_factor: float32 [256, 256], replicated, as said below
- station_rows: int32 [512, 4], replicated, may hold values from 0 to 65535
- station_weights: float32 [512, 4], replicated, may hold values from -3 to 3
- event_rows: int32 [8, 4], replicated, may hold values from 0 to 65535
- event_weights: float32 [8, 4], replicated, may hold values from -3 to 3
- mode_freq: float32 [2048], P('col'), may hold values from 0.05 to 1.5
- mode_damp: float32 [2048], P('col'), may hold values from 0.0001 to 0.005
Outputs:
- rotated: float32 [65536, 2048], P('row', 'col')
- seismograms: float32 [8, 512, 1024], P(None, 'row', 'col')
Inputs may be any that keep to these rules, and one draw needn't show every extreme that they name: panel_factor is upper triangular with a positive diagonal.
All inputs are finite; a program needn't handle non-finite values.
Results may differ from a plain program's by a relative error of at most 0.0003.
Values sent between devices are 32-bit elements; how exact they have to be, the bound alone decides.
A program may use at most 128 MiB of HBM per device.

v0:
```python
import jax
import jax.numpy as jnp
from jax import lax
from jax.sharding import PartitionSpec as P

NMODE = 2048
NT = 1024


def tap_sum(field, rows, weights, first, rows_here):
    local = rows - first
    inside = (local >= 0) & (local < rows_here)
    picked = jnp.take(field, jnp.clip(local, 0, rows_here - 1), axis=0)
    scaled = jnp.where(inside, weights, 0.0)
    return jnp.sum(picked * scaled[:, :, None], axis=1)


def mode_basis(freq, damp, times):
    return jnp.exp(-damp[:, None] * times[None, :]) * jnp.cos(freq[:, None] * times[None, :])


def shards(
    vectors,
    reflectors,
    panel_factor,
    station_rows,
    station_weights,
    event_rows,
    event_weights,
    mode_freq,
    mode_damp,
):
    high = lax.Precision.HIGHEST
    rows_here = vectors.shape[0]
    first = lax.axis_index("row") * rows_here
    comp_here = station_rows.shape[0] // lax.axis_size("row")
    events = event_rows.shape[0]
    width = reflectors.shape[1]
    partial_panel = jnp.dot(
        reflectors.T, vectors, precision=high, preferred_element_type=jnp.float32
    )
    panel, event_refl, event_vec = lax.psum(
        (
            partial_panel,
            tap_sum(reflectors, event_rows, event_weights, first, rows_here),
            tap_sum(vectors, event_rows, event_weights, first, rows_here),
        ),
        "row",
    )
    station_both = lax.psum_scatter(
        jnp.concatenate(
            [
                tap_sum(reflectors, station_rows, station_weights, first, rows_here),
                tap_sum(vectors, station_rows, station_weights, first, rows_here),
            ],
            axis=1,
        ),
        "row",
        scatter_dimension=0,
        tiled=True,
    )
    folded = jnp.dot(panel_factor, panel, precision=high, preferred_element_type=jnp.float32)
    rotated = vectors - jnp.dot(
        reflectors, folded, precision=high, preferred_element_type=jnp.float32
    )
    receivers = station_both[:, width:] - jnp.dot(
        station_both[:, :width], folded, precision=high, preferred_element_type=jnp.float32
    )
    sources = event_vec - jnp.dot(
        event_refl, folded, precision=high, preferred_element_type=jnp.float32
    )
    factor = 1.0 / float(NMODE) ** 0.5
    times = jnp.arange(NT).astype(jnp.float32)
    basis = mode_basis(mode_freq, mode_damp, times)
    amplitude = (sources[:, None, :] * receivers[None, :, :]).reshape(events * comp_here, -1)
    partial_series = jnp.dot(
        amplitude, basis, precision=high, preferred_element_type=jnp.float32
    ).reshape(events, comp_here, NT)
    seismograms = lax.psum_scatter(partial_series, "col", scatter_dimension=2, tiled=True) * factor
    return (rotated, seismograms)


def solution(mesh):
    placed = (P("row", "col"), P("row", None), P(), P(), P(), P(), P(), P("col"), P("col"))
    return jax.shard_map(
        shards,
        mesh=mesh,
        in_specs=placed,
        out_specs=(P("row", "col"), P(None, "row", "col")),
        check_vma=False,
    )
```

profile of v0, /device:TPU:1, one launch (start us, length us, event | category | flops | bytes accessed | tf_op | source)
XLA Modules:
  0.0 266.9 jit_solution(4937262338013175116)
XLA Ops:
  7.2 0.0 copy-start
  7.2 0.0 copy-start.3
  7.2 0.0 all-reduce.3.cloned.1.call-start
  7.2 19.5 %fusion.14 = f32[256,512]{1,0:T(8,128)} fusion(f32[8192,256]{1,0:T(8,128)} %param.10, f32[8192,512]{1,0:T(8,128)} %param.9), kind=kOutput, calls=%fused_computation.36 | convolution fusion | flops 12884901888 | bytes 25690112 | tf_op jit(solution)/shard_map/dot_general | solution.py:39
  26.8 0.0 all-reduce.3.cloned.1.call-update
  26.8 0.0 reduce-scatter.3.cloned.1.call-start
  26.9 0.0 copy-done.3
  26.9 0.1 copy.29
  27.0 0.2 reshape.48
  27.2 10.0 %gather_fusion.2 = f32[2048,256]{1,0:T(8,128)S(1)} fusion(f32[8192,256]{1,0:T(8,128)} %param.10, s32[2048]{0:T(1024)S(1)} %broadcast_clamp_fusion), kind=kCustom, calls=%fused_computation.2 | custom fusion | bytes 4202496 | tf_op jit(solution)/shard_map/jit(_take)/gather | solution.py:13
  37.2 0.0 copy-start.4
  37.3 15.4 %gather_fusion.3 = f32[2048,512]{1,0:T(8,128)} fusion(f32[8192,512]{1,0:T(8,128)} %param.9, s32[2048]{0:T(1024)S(1)} %broadcast_clamp_fusion), kind=kCustom, calls=%fused_computation.3 | custom fusion | bytes 8396800 | tf_op jit(solution)/shard_map/jit(_take)/gather | solution.py:13
  52.6 0.0 copy-done.4
  52.6 0.2 copy.28
  52.8 0.1 copy.30
  53.0 1.7 reshape.47
  54.6 5.2 %reshape.55 = f32[512,4,512]{2,1,0:T(4,128)} reshape(f32[2048,512]{1,0:T(8,128)} %gather_fusion.3) | data formatting | bytes 8388608 | tf_op jit(solution)/shard_map/jit(_take)/gather | solution.py:13
  59.8 0.0 copy-start.2
  59.8 6.0 %multiply_reduce_fusion = f32[512,512]{1,0:T(8,128)S(1)} fusion(f32[512,4,512]{2,1,0:T(4,128)} %reshape.55, f32[512,4]{1,0:T(8,128)S(1)} %copy.30, pred[512,4]{1,0:T(8,128)(4,1)S(1)} %copy.28), kind=kLoop, calls=%fused_computation.5 | loop fusion | flops 2883584 | bytes 5253120 | tf_op jit(solution)/shard_map/reduce_sum | solution.py:15
  65.8 0.0 copy-done.2
  65.9 0.0 copy-start.5
  65.9 0.0 copy-start.6
  65.9 0.0 copy-start.7
  65.9 3.0 %multiply_reduce_fusion.1 = f32[512,256]{1,0:T(8,128)S(1)} fusion(f32[512,4,256]{2,1,0:T(4,128)S(1)} %copy-done.2, f32[512,4]{1,0:T(8,128)S(1)} %copy.30, pred[512,4]{1,0:T(8,128)(4,1)S(1)} %copy.28), kind=kLoop, calls=%fused_computation.13 | loop fusion | flops 1441792 | bytes 2631680 | tf_op jit(solution)/shard_map/reduce_sum | solution.py:15
  68.9 0.0 copy-start.8
  68.9 1.2 pad_maximum_fusion
  70.1 0.0 reduce-scatter.3.cloned.1.call-update
  70.2 0.0 reduce-scatter.5.cloned.1.call-start
  70.2 0.0 copy-done.5
  70.2 0.1 copy.24
  70.3 0.1 reshape.32
  70.4 4.0 %gather_fusion.1 = f32[32,256]{1,0:T(8,128)S(1)} fusion(f32[8192,256]{1,0:T(8,128)} %param.10, s32[1024]{0:T(1024)S(1)} %pad_clamp_fusion), kind=kCustom, calls=%fused_computation.1 | custom fusion | bytes 65664 | tf_op jit(solution)/shard_map/jit(_take)/gather | solution.py:13
  74.4 6.4 %gather_fusion = f32[32,512]{1,0:T(8,128)S(1)} fusion(f32[8192,512]{1,0:T(8,128)} %param.9, s32[1024]{0:T(1024)S(1)} %pad_clamp_fusion), kind=kCustom, calls=%fused_computation | custom fusion | bytes 131200 | tf_op jit(solution)/shard_map/jit(_take)/gather | solution.py:13
  80.8 0.0 copy-done.6
  80.9 0.1 copy.25
  80.9 0.0 copy-done.7
  81.0 0.1 copy.23
  81.1 0.1 multiply_reduce_fusion.3
  81.2 0.1 multiply_reduce_fusion.2
  81.3 31.2 %all-reduce = (f32[8,512]{1,0:T(8,128)S(1)}, f32[8,256]{1,0:T(8,128)S(1)}) all-reduce(f32[8,512]{1,0:T(8,128)S(1)} %multiply_reduce_fusion.2, f32[8,256]{1,0:T(8,128)S(1)} %multiply_reduce_fusion.3), channel_id=1, replica_groups=mesh['row'=8,'col'=4] {'row'}, use_global_device_ids=true, to_apply=%region_2.3 | all-reduce | flops 6144 | bytes 49152 | tf_op jit(solution)/shard_map/psum | solution.py:42
  112.6 0.0 all-reduce.3.cloned.1.call-done
  112.6 0.0 copy-done
  112.6 2.0 fusion.15
  114.6 0.5 convolution_subtract_fusion.1
  115.2 53.9 %reduce-scatter.3.cloned.1.call-done = f32[64,768]{1,0:T(8,128)} async-done(((f32[512,768]{1,0:T(8,128)}), f32[64,768]{1,0:T(8,128)}) %reduce-scatter.3.cloned.1.call-update) | async-done | bytes 196624 | tf_op jit(solution)/shard_map/reduce_scatter | solution.py:50
  169.1 1.6 convolution_subtract_fusion
  170.6 0.0 copy-done.8
  170.7 12.1 %fusion = f32[8,64,1024]{2,1,0:T(8,128)} fusion(f32[512]{0:T(512)S(1)} %copy-done.8, f32[1024]{0:T(1024)S(1)} %iota_convert_fusion, f32[512]{0:T(512)S(1)} %neg.4, f32[64,512]{1,0:T(8,128)S(1)} %convolution_subtract_fusion, f32[8,512]{1,0:T(8,128)S(1)} %convolution_subtract_fusion.1), kind=kOutput, calls=%fused_computation.6 | convolution fusion | flops 3223060480 | bytes 2252800 | tf_op jit(solution)/shard_map/dot_general | solution.py:76
  182.7 0.0 reduce-scatter.5.cloned.1.call-update
  182.7 17.6 %copy.22 = f32[8192,512]{0,1:T(8,128)} copy(f32[8192,512]{1,0:T(8,128)} %param.9) | data formatting | bytes 33554432 | tf_op args[0]
  200.3 40.7 %bitcast_subtract_fusion = f32[8192,512]{0,1:T(8,128)} fusion(f32[8192,512]{0,1:T(8,128)} %copy.22, f32[512,256]{1,0:T(8,128)S(1)} %fusion.15, f32[8192,256]{1,0:T(8,128)} %param.10), kind=kOutput, calls=%fused_computation.4 | convolution fusion | flops 12889096192 | bytes 42467328 | tf_op jit(solution)/shard_map/dot_general | solution.py:63
  241.0 0.0 copy-start.1
  241.0 17.5 %copy.33 = f32[8192,512]{1,0:T(8,128)} copy(f32[8192,512]{0,1:T(8,128)} %bitcast_subtract_fusion) | data formatting | bytes 33554432
  258.5 0.0 reduce-scatter.5.cloned.1.call-done
  258.5 1.9 broadcast_multiply_fusion
  260.4 0.0 copy-done.1
  (10 shorter events, 0.1 us)
Async XLA Ops:
  7.2 105.4 %copy-start = (f32[256,256]{1,0:T(8,128)S(1)}, f32[256,256]{1,0:T(8,128)}, u32[]{:S(2)}) copy-start(f32[256,256]{1,0:T(8,128)} %param.11) | copy-start | bytes 786436
  7.2 19.7 %copy-start.3 = (s32[512,4]{0,1:T(4,128)S(1)}, s32[512,4]{0,1:T(4,128)}, u32[]{:S(2)}) copy-start(s32[512,4]{0,1:T(4,128)} %param.12) | copy-start | bytes 24580
  7.2 105.4 %all-reduce.3.cloned.1.call-start = ((), (), s32[]{:S(2)}) async-start(), calls=%async_computation.2 | async-start | bytes 1048576 | tf_op jit(solution)/shard_map/psum | solution.py:42
  26.8 142.3 %reduce-scatter.3.cloned.1.call-start = ((), (), s32[]{:S(2)}) async-start(), calls=%async_computation.3 | async-start | bytes 1769472 | tf_op jit(solution)/shard_map/reduce_scatter | solution.py:50
  37.2 15.4 %copy-start.4 = (f32[512,4]{0,1:T(4,128)S(1)}, f32[512,4]{0,1:T(4,128)}, u32[]{:S(2)}) copy-start(f32[512,4]{0,1:T(4,128)} %param.13) | copy-start | bytes 24580
  59.8 6.0 %copy-start.2 = (f32[512,4,256]{2,1,0:T(4,128)S(1)}, f32[512,4,256]{2,1,0:T(4,128)}, u32[]{:S(2)}) copy-start(f32[512,4,256]{2,1,0:T(4,128)} %reshape.47) | copy-start | bytes 6291460
  65.9 4.4 %copy-start.5 = (s32[8,4]{0,1:T(4,128)S(1)}, s32[8,4]{0,1:T(4,128)}, u32[]{:S(2)}) copy-start(s32[8,4]{0,1:T(4,128)} %param.14) | copy-start | bytes 388
  65.9 15.0 %copy-start.6 = (f32[8,4]{0,1:T(4,128)S(1)}, f32[8,4]{0,1:T(4,128)}, u32[]{:S(2)}) copy-start(f32[8,4]{0,1:T(4,128)} %param.15) | copy-start | bytes 388
  65.9 15.1 %copy-start.7 = (f32[512]{0:T(512)S(1)}, f32[512]{0:T(512)}, u32[]{:S(2)}) copy-start(f32[512]{0:T(512)} %param.17) | copy-start | bytes 6148
  68.9 101.8 %copy-start.8 = (f32[512]{0:T(512)S(1)}, f32[512]{0:T(512)}, u32[]{:S(2)}) copy-start(f32[512]{0:T(512)} %param.16) | copy-start | bytes 6148
  70.2 188.3 %reduce-scatter.5.cloned.1.call-start = ((), (), s32[]{:S(2)}) async-start(), calls=%async_computation.4 | async-start | bytes 2621440 | tf_op jit(solution)/shard_map/reduce_scatter | solution.py:79
  241.0 19.4 %copy-start.1 = (f32[256,256]{1,0:T(8,128)S(1)}, f32[256,256]{1,0:T(8,128)}, u32[]{:S(2)}) copy-start(f32[256,256]{1,0:T(8,128)} %param.11) | copy-start | bytes 786436
Sparse Core Ops, SparseCore 0:
  26.9 72.8 all-reduce.2
  104.2 64.8 reduce-scatter.2
  182.9 31.5 reduce-scatter.4
where the time goes:
time: 270 us; the launch traced here: 267 us
  local copies, waits for them, and re-layouts  78.8 us (29%)
  matrix products  76.4 us (28%)
  waiting for transfers between devices  54 us (20%)
  blocking collectives  31.2 us (12%)
  between operations  14 us (5%)
  other arithmetic  12.4 us (5%)
    reduce_scatter x1, waiting for transfers between devices, shards(): lax.psum_scatter(jnp.concatenate([tap_sum(reflectors, station_rows, stati...  53.9 us
    gather x8, local copies, waits for them, and re-layouts, tap_sum(): picked = jnp.take(field, jnp.clip(local, 0, rows_here - 1), axis=0)  42.7 us
    dot_general x1, matrix products, shards(): jnp.dot(reflectors, folded, precision=high, preferred_element_type=jnp.fl...  40.7 us
    unnamed x20, local copies, waits for them, and re-layouts  35.1 us
    psum x1, blocking collectives, shards(): lax.psum((partial_panel, tap_sum(reflectors, event_rows, event_weights, f...  31.2 us
    dot_general x1, matrix products, shards(): jnp.dot(reflectors.T, vectors, precision=high, preferred_element_type=jnp...  19.5 us
    dot_general x1, matrix products, shards(): jnp.dot(amplitude, basis, precision=high, preferred_element_type=jnp.floa...  12.1 us
    reduce_sum x4, other arithmetic, tap_sum(): return jnp.sum(picked * scaled[:, :, None], axis=1)  9.21 us
  transfers between devices with their start and end apart: 3, of which 1 were waited for; matrix products, arithmetic and copies ran while one was open for 50% of the time, Pallas kernels for 0%

commit v1 on v0

v1 whole, which is shorter than its diff:
```python
import functools
import math

import jax
import jax.numpy as jnp
import numpy as np
from jax import lax
from jax.experimental import pallas as pl
from jax.experimental.pallas import tpu as pltpu
from jax.sharding import PartitionSpec as P

MESH = pl.DeviceIdType.MESH
F32 = jnp.float32
BF16 = jnp.bfloat16
GROUP = 4
PARTS = 2

TURN_A = 6.28125
TURN_B = float(np.round((2 * math.pi - TURN_A) * 2**20) / 2**20)
TURN_C = 2 * math.pi - TURN_A - TURN_B


def cos_series():
    square = np.linspace(0.0, (1.01 * math.pi) ** 2, 4001)
    fit = np.polynomial.Chebyshev.fit(square, np.cos(np.sqrt(square)), 7)
    return [float(c) for c in fit.convert(kind=np.polynomial.Polynomial).coef]


COS = cos_series()


def cosine(x):
    turns = jnp.floor(x * (0.5 / math.pi) + 0.5)
    rest = ((x - turns * TURN_A) - turns * TURN_B) - turns * TURN_C
    square = rest * rest
    total = jnp.full_like(square, COS[-1])
    for coefficient in COS[-2::-1]:
        total = total * square + coefficient
    return total


def split(x):
    high = x.astype(BF16)
    return high, (x - high.astype(F32)).astype(BF16)


def dot3(a, b, over):
    dims = (((over[0],), (over[1],)), ((), ()))
    dot = functools.partial(lax.dot_general, dimension_numbers=dims, preferred_element_type=F32)
    return dot(a[0], b[0]) + (dot(a[0], b[1]) + dot(a[1], b[0]))


def panel_kernel(
    sizes,
    taps_ref,
    weights_ref,
    vec_hbm,
    refl_hbm,
    factor_ref,
    modes_ref,
    high_ref,
    low_ref,
    seis_ref,
    vec,
    refl,
    part,
    part_got,
    mine,
    mine_got,
    panel,
    whole,
    picked,
    picked_refl,
    sums,
    sums_got,
    block,
    block_got,
    every,
    every_modes,
    basis_high,
    basis_low,
    load_sem,
    send1,
    recv1,
    send2,
    recv2,
    send3,
    recv3,
    send4,
    recv4,
    send5,
    recv5,
    send6,
    recv6,
    send7,
    recv7,
):
    groups, cols, chunk, chunks, taps, comp, events, samples = sizes
    row, col = lax.axis_index("row"), lax.axis_index("col")
    group, place = row // GROUP, lax.rem(row, GROUP)
    width = refl.shape[1]

    def mate(o):
        return (group * GROUP + lax.rem(place + o, GROUP), col)

    def across(o):
        return (lax.rem(group + o, groups) * GROUP + place, col)

    def beside(o):
        return (row, lax.rem(col + o, cols))

    def send(src, dst, sems, where):
        return pltpu.make_async_remote_copy(
            src_ref=src,
            dst_ref=dst,
            send_sem=sems[0],
            recv_sem=sems[1],
            device_id=where,
            device_id_type=MESH,
        )

    def load(i, start):
        at = pl.ds(pl.multiple_of(i * chunk, chunk), chunk)
        for k, (src, dst) in enumerate(((refl_hbm, refl), (vec_hbm, vec))):
            copy = pltpu.make_async_copy(src.at[at], dst.at[at], load_sem.at[i, k])
            copy.start() if start else copy.wait()

    for i in range(chunks):
        load(i, True)
    barrier = pltpu.get_barrier_semaphore()
    others = (
        [mate(o) for o in range(1, GROUP)]
        + [across(o) for o in range(1, groups)]
        + [beside(o) for o in range(1, cols)]
    )
    for other in others:
        pl.semaphore_signal(barrier, inc=1, device_id=other, device_id_type=MESH)

    panel[...] = jnp.zeros_like(panel)

    @pl.loop(0, chunks)
    def _(i):
        load(i, False)
        at = pl.ds(pl.multiple_of(i * chunk, chunk), chunk)
        panel[...] += dot3(split(refl[at, :]), split(vec[at, :]), (0, 0))

    part[...] = panel[...].reshape(part.shape)
    pl.semaphore_wait(barrier, len(others))

    first = [
        [
            send(
                part.at[h, lax.rem(place + o, GROUP)],
                part_got.at[h, o - 1],
                (send1.at[h, o - 1], recv1.at[h, o - 1]),
                mate(o),
            )
            for o in range(1, GROUP)
        ]
        for h in range(PARTS)
    ]
    for copies in first:
        for copy in copies:
            copy.start()
    wave = [
        send(
            modes_ref,
            every_modes.at[col],
            (send7.at[o - 1], recv7.at[o - 1]),
            beside(o),
        )
        for o in range(1, cols)
    ]
    for copy in wave:
        copy.start()

    total = groups * GROUP * comp + events

    def gather(begin, end):
        @pl.loop(begin, end)
        def _(c8):
            for u in range(8):
                c = c8 * 8 + u
                a, b = None, None
                for j in range(taps):
                    at = taps_ref[c * taps + j]
                    scale = weights_ref[c * taps + j]
                    x = vec[pl.ds(at, 1), :] * scale
                    y = refl[pl.ds(at, 1), :] * scale
                    a = x if a is None else a + x
                    b = y if b is None else b + y
                picked[pl.ds(c, 1), :] = a
                picked_refl[pl.ds(c, 1), :] = b

    third = total // 8 // 3
    gather(0, third)
    second = []
    for h in range(PARTS):
        for copy in first[h]:
            copy.wait()
        value = part[h, place]
        for o in range(1, GROUP):
            value = value + part_got[h, o - 1]
        mine[h] = value
        second.append(
            [
                send(
                    mine.at[h],
                    mine_got.at[h, o - 1],
                    (send2.at[h, o - 1], recv2.at[h, o - 1]),
                    across(o),
                )
                for o in range(1, groups)
            ]
        )
        for copy in second[h]:
            copy.start()
    gather(third, 2 * third)
    back = []
    for h in range(PARTS):
        for copy in second[h]:
            copy.wait()
        value = mine[h]
        for o in range(1, groups):
            value = value + mine_got[h, o - 1]
        whole[h, place] = value
        back.append(
            [
                send(
                    whole.at[h, place],
                    whole.at[h, place],
                    (send3.at[h, o - 1], recv3.at[h, o - 1]),
                    mate(o),
                )
                for o in range(1, GROUP)
            ]
        )
        for copy in back[h]:
            copy.start()
    gather(2 * third, total // 8)
    for h in range(PARTS):
        for copy in back[h]:
            copy.wait()
    folded = dot3(split(factor_ref[...]), split(whole[...].reshape(panel.shape)), (1, 0))
    high, low = split(folded)
    high_ref[...] = high
    low_ref[...] = low

    source = picked[groups * GROUP * comp :, :] - dot3(
        split(picked_refl[groups * GROUP * comp :, :]), (high, low), (1, 0)
    )
    for g in range(groups):
        at = slice(g * GROUP * comp, (g + 1) * GROUP * comp)
        value = picked[at, :] - dot3(split(picked_refl[at, :]), (high, low), (1, 0))
        for q in range(GROUP):
            sums[q, g, :comp, :] = value[q * comp : (q + 1) * comp, :]
            sums[q, g, comp:, :] = source
    copies = [
        send(
            sums.at[lax.rem(place + o, GROUP)],
            sums_got.at[o - 1],
            (send4.at[o - 1], recv4.at[o - 1]),
            mate(o),
        )
        for o in range(1, GROUP)
    ]
    for copy in copies:
        copy.start()

    every_modes[col] = modes_ref[...]
    for copy in wave:
        copy.wait()
    step = min(samples, 32)
    for c in range(cols):
        freq, damp = every_modes[c, 0:1, :], every_modes[c, 1:2, :]

        @pl.loop(0, samples // step)
        def _(i):
            begin = pl.multiple_of(i * step, step)
            shape = (step, freq.shape[1])
            times = (lax.broadcasted_iota(jnp.int32, shape, 0) + (col * samples + begin)).astype(F32)
            value = jnp.exp(-damp * times) * cosine(freq * times)
            basis_high[c, pl.ds(begin, step), :], basis_low[c, pl.ds(begin, step), :] = split(value)

    for copy in copies:
        copy.wait()
    value = sums[place]
    for o in range(1, GROUP):
        value = value + sums_got[o - 1]
    block[...] = value
    copies = [
        send(
            block.at[lax.rem(group + o, groups)],
            block_got.at[o - 1],
            (send5.at[o - 1], recv5.at[o - 1]),
            across(o),
        )
        for o in range(1, groups)
    ]
    for copy in copies:
        copy.start()
    for copy in copies:
        copy.wait()
    value = block[group]
    for o in range(1, groups):
        value = value + block_got[o - 1]
    every[col] = value
    copies = [
        send(
            every.at[col],
            every.at[col],
            (send6.at[o - 1], recv6.at[o - 1]),
            beside(o),
        )
        for o in range(1, cols)
    ]
    for copy in copies:
        copy.start()
    for copy in copies:
        copy.wait()

    result = None
    for c in range(cols):
        receivers = every[c, :comp, :]
        amplitude = jnp.concatenate(
            [every[c, comp + e : comp + e + 1, :] * receivers for e in range(events)], axis=0
        )
        value = dot3(split(amplitude), (basis_high[c], basis_low[c]), (1, 1))
        result = value if result is None else result + value
    scale = 1.0 / float(cols * vec.shape[1]) ** 0.5
    seis_ref[...] = (result * scale).reshape(seis_ref.shape)


def update_kernel(vec_ref, refl_ref, high_ref, low_ref, out_ref):
    folded = (high_ref[...], low_ref[...])
    out_ref[...] = vec_ref[...] - dot3(split(refl_ref[...]), folded, (1, 0))


def shards(
    rows,
    cols,
    vectors,
    reflectors,
    panel_factor,
    station_rows,
    station_weights,
    event_rows,
    event_weights,
    mode_freq,
    mode_damp,
):
    here, wide = vectors.shape
    width = reflectors.shape[1]
    comps, taps = station_rows.shape
    events = event_rows.shape[0]
    comp = comps // rows
    samples = 1024 // cols
    groups = rows // GROUP
    chunk = min(1024, here)
    chunks = here // chunk

    local = jnp.concatenate([station_rows, event_rows]).reshape(-1) - lax.axis_index("row") * here
    weights = jnp.concatenate([station_weights, event_weights]).reshape(-1)
    weights = jnp.where((local >= 0) & (local < here), weights, 0.0)
    local = jnp.clip(local, 0, here - 1)
    modes = jnp.pad(jnp.stack([mode_freq, mode_damp]), ((0, 6), (0, 0)))

    piece = width // PARTS // GROUP
    tall = comp + events
    dma = pltpu.SemaphoreType.DMA
    out_groups, out_cols = max(groups - 1, 1), max(cols - 1, 1)
    in_vmem = pl.BlockSpec(memory_space=pltpu.VMEM)
    in_smem = pl.BlockSpec(memory_space=pltpu.SMEM)
    in_any = pl.BlockSpec(memory_space=pl.ANY)
    sizes = (groups, cols, chunk, chunks, taps, comp, events, samples)
    high, low, seismograms = pl.pallas_call(
        functools.partial(panel_kernel, sizes),
        out_shape=(
            jax.ShapeDtypeStruct((width, wide), BF16),
            jax.ShapeDtypeStruct((width, wide), BF16),
            jax.ShapeDtypeStruct((events, comp, samples), F32),
        ),
        in_specs=[in_smem, in_smem, in_any, in_any, in_vmem, in_vmem],
        out_specs=(in_vmem, in_vmem, in_vmem),
        scratch_shapes=[
            pltpu.VMEM((here, wide), F32),
            pltpu.VMEM((here, width), F32),
            pltpu.VMEM((PARTS, GROUP, piece, wide), F32),
            pltpu.VMEM((PARTS, GROUP - 1, piece, wide), F32),
            pltpu.VMEM((PARTS, piece, wide), F32),
            pltpu.VMEM((PARTS, out_groups, piece, wide), F32),
            pltpu.VMEM((width, wide), F32),
            pltpu.VMEM((PARTS, GROUP, piece, wide), F32),
            pltpu.VMEM((comps + events, wide), F32),
            pltpu.VMEM((comps + events, width), F32),
            pltpu.VMEM((GROUP, groups, tall, wide), F32),
            pltpu.VMEM((GROUP - 1, groups, tall, wide), F32),
            pltpu.VMEM((groups, tall, wide), F32),
            pltpu.VMEM((out_groups, tall, wide), F32),
            pltpu.VMEM((cols, tall, wide), F32),
            pltpu.VMEM((cols, 8, wide), F32),
            pltpu.VMEM((cols, samples, wide), BF16),
            pltpu.VMEM((cols, samples, wide), BF16),
            dma((chunks, 2)),
            dma((PARTS, GROUP - 1)),
            dma((PARTS, GROUP - 1)),
            dma((PARTS, out_groups)),
            dma((PARTS, out_groups)),
            dma((PARTS, GROUP - 1)),
            dma((PARTS, GROUP - 1)),
            dma((GROUP - 1,)),
            dma((GROUP - 1,)),
            dma((out_groups,)),
            dma((out_groups,)),
            dma((out_cols,)),
            dma((out_cols,)),
            dma((out_cols,)),
            dma((out_cols,)),
        ],
        compiler_params=pltpu.CompilerParams(
            collective_id=0, has_side_effects=True, vmem_limit_bytes=48 * 2**20
        ),
        cost_estimate=pl.CostEstimate(
            flops=6 * here * width * wide,
            bytes_accessed=4 * here * (wide + width),
            transcendentals=0,
        ),
    )(local, weights, vectors, reflectors, panel_factor, modes)

    tile = min(1024, here)
    rotated = pl.pallas_call(
        update_kernel,
        grid=(here // tile,),
        out_shape=jax.ShapeDtypeStruct((here, wide), F32),
        in_specs=[
            pl.BlockSpec((tile, wide), lambda i: (i, 0)),
            pl.BlockSpec((tile, width), lambda i: (i, 0)),
            pl.BlockSpec((width, wide), lambda i: (0, 0)),
            pl.BlockSpec((width, wide), lambda i: (0, 0)),
        ],
        out_specs=pl.BlockSpec((tile, wide), lambda i: (i, 0)),
        compiler_params=pltpu.CompilerParams(vmem_limit_bytes=32 * 2**20),
        cost_estimate=pl.CostEstimate(
            flops=6 * here * width * wide,
            bytes_accessed=4 * here * (2 * wide + width),
            transcendentals=0,
        ),
    )(vectors, reflectors, high, low)
    return (rotated, seismograms)


def solution(mesh):
    placed = (P("row", "col"), P("row", None), P(), P(), P(), P(), P(), P("col"), P("col"))
    return jax.shard_map(
        functools.partial(shards, mesh.shape["row"], mesh.shape["col"]),
        mesh=mesh,
        in_specs=placed,
        out_specs=(P("row", "col"), P(None, "row", "col")),
        check_vma=False,
    )
```

time: 270 us -> 87.1 us (0.32); the launches traced: 267 us -> 86.7 us
  Pallas kernels: 0 us -> 81.5 us
  local copies, waits for them, and re-layouts: 78.8 us -> 2.37 us
  matrix products: 76.4 us -> 0 us
  waiting for transfers between devices: 54 us -> 0 us
  blocking collectives: 31.2 us -> 0 us
  between operations: 14 us -> 0.69 us
  other arithmetic: 12.4 us -> 2.18 us
    pallas_call x0 -> x2, Pallas kernels: none -> 81.5 us  [the longest x1 64.3 us: shards(): pl.pallas_call(functools.partial(panel_kernel, sizes), out_shape=(jax.Sha...]
    dot_general x6 -> x0, matrix products: 76.4 us -> none  [the longest x1 40.7 us: shards(): jnp.dot(reflectors, folded, precision=high, preferred_element_type=jnp.fl...]
    reduce_scatter x2 -> x0, waiting for transfers between devices: 53.9 us -> none  [the longest x1 53.9 us: shards(): lax.psum_scatter(jnp.concatenate([tap_sum(reflectors, station_rows, stati...]
    gather x8 -> x0, local copies, waits for them, and re-layouts: 42.7 us -> none  [tap_sum(): picked = jnp.take(field, jnp.clip(local, 0, rows_here - 1), axis=0)]
    unnamed x20 -> x5, local copies, waits for them, and re-layouts: 35.1 us -> 1.74 us
    psum x1 -> x0, blocking collectives: 31.2 us -> none  [shards(): lax.psum((partial_panel, tap_sum(reflectors, event_rows, event_weights, f...]
    reduce_sum x4 -> x0, other arithmetic: 9.21 us -> none  [tap_sum(): return jnp.sum(picked * scaled[:, :, None], axis=1)]
  transfers between devices with their start and end apart: 3 -> 0, of which waited for: 1 -> 0; matrix products, arithmetic and copies ran while one was open for 50% -> 0% of each run, Pallas kernels for 0% -> 0%
where the time goes in v1:
time: 87.1 us; the launch traced here: 86.7 us
  Pallas kernels  81.5 us (94%)
  local copies, waits for them, and re-layouts  2.37 us (3%)
  other arithmetic  2.18 us (3%)
    pallas_call x1, Pallas kernels, shards(): pl.pallas_call(functools.partial(panel_kernel, sizes), out_shape=(jax.Sha...  64.3 us
    pallas_call x1, Pallas kernels, shards(): pl.pallas_call(update_kernel, grid=(here // tile,), out_shape=jax.ShapeDt...  17.2 us

profile of v1, /device:TPU:1, one launch (start us, length us, event | category | flops | bytes accessed | tf_op | source)
XLA Modules:
  0.0 86.7 jit_solution(269061756688881912)
XLA Ops:
  0.6 0.8 maximum_select_fusion
  1.4 0.7 fusion
  2.1 0.7 select_maximum_fusion.modes_ref
  2.8 0.1 copy.11
  3.0 0.2 min.12.taps_ref
  3.1 0.1 copy.12
  3.3 0.2 select_n.7.weights_ref
  3.5 0.0 copy-start.1
  3.5 0.9 %copy-done.1 = f32[256,256]{1,0:T(8,128)S(1)} copy-done((f32[256,256]{1,0:T(8,128)S(1)}, f32[256,256]{1,0:T(8,128)}, u32[]{:S(2)}) %copy-start.1) | copy-done | bytes 262168
  4.4 0.0 copy-start
  4.4 64.3 %shard_map.104 = (bf16[256,512]{1,0:T(8,128)(2,1)S(1)}, bf16[256,512]{1,0:T(8,128)(2,1)S(1)}, f32[8,64,256]{2,1,0:T(8,128)S(1)}) custom-call(s32[2080]{0:T(1024)S(1)} %min.12.taps_ref, f32[2080]{0:T(1024)S(1)} %select_n.7.weights_ref, f32[8192,512]{1,0:T(8,128)} %vec_ref.1, f32[8192,256]{1,0:T(8,128)} %refl_ref.1, f32[256,256]{1,0:T(8,128)S(1)} %copy-done.1, ...), custom_call_target="tpu_custom_call" | custom-call | flops 6442450944 | bytes 25165824 | tf_op jit(solution)/shard_map/pallas_call | solution.py:376
  68.7 0.0 copy-done
  68.8 17.2 %shard_map.105 = f32[8192,512]{1,0:T(8,128)} custom-call(f32[8192,512]{1,0:T(8,128)} %vec_ref.1, f32[8192,256]{1,0:T(8,128)S(1)} %copy-done, bf16[256,512]{1,0:T(8,128)(2,1)S(1)} %get-tuple-element.5.high_ref, bf16[256,512]{1,0:T(8,128)(2,1)S(1)} %get-tuple-element.6.low_ref), custom_call_target="tpu_custom_call" | custom-call | flops 6442450944 | bytes 41943040 | tf_op jit(solution)/shard_map/pallas_call | solution.py:431
  86.0 0.8 copy.14
Async XLA Ops:
  3.5 1.0 %copy-start.1 = (f32[256,256]{1,0:T(8,128)S(1)}, f32[256,256]{1,0:T(8,128)}, u32[]{:S(2)}) copy-start(f32[256,256]{1,0:T(8,128)} %factor_ref.1) | copy-start | bytes 786436
  4.4 64.3 %copy-start = (f32[8192,256]{1,0:T(8,128)S(1)}, f32[8192,256]{1,0:T(8,128)}, u32[]{:S(2)}) copy-start(f32[8192,256]{1,0:T(8,128)} %refl_ref.1) | copy-start | bytes 25165828

commit v2 on v1

v2 whole, which is shorter than its diff:
```python
import functools
import math

import jax
import jax.numpy as jnp
import numpy as np
from jax import lax
from jax.experimental import pallas as pl
from jax.experimental.pallas import tpu as pltpu
from jax.sharding import PartitionSpec as P

MESH = pl.DeviceIdType.MESH
F32 = jnp.float32
BF16 = jnp.bfloat16
GROUP = 4

TURN_A = 6.28125
TURN_B = float(np.round((2 * math.pi - TURN_A) * 2**20) / 2**20)
TURN_C = 2 * math.pi - TURN_A - TURN_B


def cos_series():
    square = np.linspace(0.0, (1.01 * math.pi) ** 2, 4001)
    fit = np.polynomial.Chebyshev.fit(square, np.cos(np.sqrt(square)), 7)
    return [float(c) for c in fit.convert(kind=np.polynomial.Polynomial).coef]


COS = cos_series()


def cosine(x):
    turns = jnp.floor(x * (0.5 / math.pi) + 0.5)
    rest = ((x - turns * TURN_A) - turns * TURN_B) - turns * TURN_C
    square = rest * rest
    total = jnp.full_like(square, COS[-1])
    for coefficient in COS[-2::-1]:
        total = total * square + coefficient
    return total


def split(x):
    high = x.astype(BF16)
    return high, (x - high.astype(F32)).astype(BF16)


def dot3(a, b, over):
    dims = (((over[0],), (over[1],)), ((), ()))
    dot = functools.partial(lax.dot_general, dimension_numbers=dims, preferred_element_type=F32)
    return dot(a[0], b[0]) + (dot(a[0], b[1]) + dot(a[1], b[0]))


def panel_kernel(
    sizes,
    taps_ref,
    weights_ref,
    vec_hbm,
    refl_hbm,
    factor_hbm,
    freq_hbm,
    damp_hbm,
    vec,
    seis_ref,
    refl,
    freq_row,
    damp_row,
    factor,
    modes_ref,
    high_ref,
    low_ref,
    part,
    part_got,
    mine,
    mine_got,
    panel,
    whole,
    picked,
    picked_refl,
    sums,
    sums_got,
    block,
    block_got,
    every,
    every_modes,
    basis_high,
    basis_low,
    load_sem,
    small_sem,
    send1,
    recv1,
    send2,
    recv2,
    send3,
    recv3,
    send4,
    recv4,
    send5,
    recv5,
    send6,
    recv6,
    send7,
    recv7,
):
    parts, groups, cols, chunk, chunks, taps, comp, events, samples = sizes
    row, col = lax.axis_index("row"), lax.axis_index("col")
    group, place = row // GROUP, lax.rem(row, GROUP)
    width = refl.shape[1]

    def mate(o):
        return (group * GROUP + lax.rem(place + o, GROUP), col)

    def across(o):
        return (lax.rem(group + o, groups) * GROUP + place, col)

    def beside(o):
        return (row, lax.rem(col + o, cols))

    def send(src, dst, sems, where):
        return pltpu.make_async_remote_copy(
            src_ref=src,
            dst_ref=dst,
            send_sem=sems[0],
            recv_sem=sems[1],
            device_id=where,
            device_id_type=MESH,
        )

    lanes = vec.shape[1] // parts

    def loads(h, i):
        at = pl.ds(pl.multiple_of(i * chunk, chunk), chunk)
        here = pl.ds(h * lanes, lanes)
        found = [pltpu.make_async_copy(vec_hbm.at[at, here], vec.at[at, here], load_sem.at[i, h])]
        if h == 0:
            found.append(pltpu.make_async_copy(refl_hbm.at[at], refl.at[at], load_sem.at[i, parts]))
        return found

    for h in range(parts):
        for i in range(chunks):
            for copy in loads(h, i):
                copy.start()
    small = [
        pltpu.make_async_copy(src, dst, small_sem.at[k])
        for k, (src, dst) in enumerate(
            ((factor_hbm, factor), (freq_hbm, freq_row), (damp_hbm, damp_row))
        )
    ]
    for copy in small:
        copy.start()
    barrier = pltpu.get_barrier_semaphore()
    others = (
        [mate(o) for o in range(1, GROUP)]
        + [across(o) for o in range(1, groups)]
        + [beside(o) for o in range(1, cols)]
    )
    for other in others:
        pl.semaphore_signal(barrier, inc=1, device_id=other, device_id_type=MESH)

    first = []
    for h in range(parts):
        panel[...] = jnp.zeros_like(panel)

        @pl.loop(0, chunks)
        def _(i):
            for copy in loads(h, i):
                copy.wait()
            at = pl.ds(pl.multiple_of(i * chunk, chunk), chunk)
            here = slice(h * lanes, (h + 1) * lanes)
            panel[...] += dot3(split(refl[at, :]), split(vec[at, here]), (0, 0))

        part[h] = panel[...].reshape(part.shape[1:])
        if h == 0:
            pl.semaphore_wait(barrier, len(others))
        first.append(
            [
                send(
                    part.at[h, lax.rem(place + o, GROUP)],
                    part_got.at[h, o - 1],
                    (send1.at[h, o - 1], recv1.at[h, o - 1]),
                    mate(o),
                )
                for o in range(1, GROUP)
            ]
        )
        for copy in first[h]:
            copy.start()
    for copy in small:
        copy.wait()
    modes_ref[...] = jnp.zeros_like(modes_ref)
    modes_ref[0:1, :] = freq_row[...]
    modes_ref[1:2, :] = damp_row[...]
    wave = [
        send(
            modes_ref,
            every_modes.at[col],
            (send7.at[o - 1], recv7.at[o - 1]),
            beside(o),
        )
        for o in range(1, cols)
    ]
    for copy in wave:
        copy.start()

    total = groups * GROUP * comp + events

    def gather(begin, end):
        @pl.loop(begin, end)
        def _(c8):
            for u in range(8):
                c = c8 * 8 + u
                a, b = None, None
                for j in range(taps):
                    at = taps_ref[c * taps + j]
                    scale = weights_ref[c * taps + j]
                    x = vec[pl.ds(at, 1), :] * scale
                    y = refl[pl.ds(at, 1), :] * scale
                    a = x if a is None else a + x
                    b = y if b is None else b + y
                picked[pl.ds(c, 1), :] = a
                picked_refl[pl.ds(c, 1), :] = b

    third = total // 8 // 3
    gather(0, third)
    second = []
    for h in range(parts):
        for copy in first[h]:
            copy.wait()
        value = part[h, place]
        for o in range(1, GROUP):
            value = value + part_got[h, o - 1]
        mine[h] = value
        second.append(
            [
                send(
                    mine.at[h],
                    mine_got.at[h, o - 1],
                    (send2.at[h, o - 1], recv2.at[h, o - 1]),
                    across(o),
                )
                for o in range(1, groups)
            ]
        )
        for copy in second[h]:
            copy.start()
    gather(third, 2 * third)
    back = []
    for h in range(parts):
        for copy in second[h]:
            copy.wait()
        value = mine[h]
        for o in range(1, groups):
            value = value + mine_got[h, o - 1]
        whole[h, place] = value
        back.append(
            [
                send(
                    whole.at[h, place],
                    whole.at[h, place],
                    (send3.at[h, o - 1], recv3.at[h, o - 1]),
                    mate(o),
                )
                for o in range(1, GROUP)
            ]
        )
        for copy in back[h]:
            copy.start()
    gather(2 * third, total // 8)
    for h in range(parts):
        for copy in back[h]:
            copy.wait()
    upper = split(factor[...])
    for h in range(parts):
        here = slice(h * lanes, (h + 1) * lanes)
        folded = dot3(upper, split(whole[h].reshape(panel.shape)), (1, 0))
        high_ref[:, here], low_ref[:, here] = split(folded)
    high, low = high_ref[...], low_ref[...]

    source = picked[groups * GROUP * comp :, :] - dot3(
        split(picked_refl[groups * GROUP * comp :, :]), (high, low), (1, 0)
    )
    for g in range(groups):
        at = slice(g * GROUP * comp, (g + 1) * GROUP * comp)
        value = picked[at, :] - dot3(split(picked_refl[at, :]), (high, low), (1, 0))
        for q in range(GROUP):
            sums[q, g, :events, :] = source
            sums[q, g, events:, :] = value[q * comp : (q + 1) * comp, :]
    spans = ((0, events + comp // 2), (events + comp // 2, comp - comp // 2))
    within = []
    for h, (low_row, tall) in enumerate(spans):
        at = pl.ds(low_row, tall)
        within.append(
            [
                send(
                    sums.at[lax.rem(place + o, GROUP), :, at],
                    sums_got.at[o - 1, :, at],
                    (send4.at[h, o - 1], recv4.at[h, o - 1]),
                    mate(o),
                )
                for o in range(1, GROUP)
            ]
        )
        for copy in within[h]:
            copy.start()

    def update(begin, end):
        @pl.loop(begin, end)
        def _(i):
            at = pl.ds(pl.multiple_of(i * chunk, chunk), chunk)
            vec[at, :] = vec[at, :] - dot3(split(refl[at, :]), (high_ref[...], low_ref[...]), (1, 0))

    every_modes[col] = modes_ref[...]
    for copy in wave:
        copy.wait()
    update(0, chunks // 2)
    step = min(samples, 32)
    for c in range(cols):
        freq, damp = every_modes[c, 0:1, :], every_modes[c, 1:2, :]

        @pl.loop(0, samples // step)
        def _(i):
            begin = pl.multiple_of(i * step, step)
            shape = (step, freq.shape[1])
            times = (lax.broadcasted_iota(jnp.int32, shape, 0) + (col * samples + begin)).astype(F32)
            value = jnp.exp(-damp * times) * cosine(freq * times)
            basis_high[c, pl.ds(begin, step), :], basis_low[c, pl.ds(begin, step), :] = split(value)

    over = []
    for h, (low_row, tall) in enumerate(spans):
        at = pl.ds(low_row, tall)
        for copy in within[h]:
            copy.wait()
        value = sums[place, :, at]
        for o in range(1, GROUP):
            value = value + sums_got[o - 1, :, at]
        block[:, at] = value
        over.append(
            [
                send(
                    block.at[lax.rem(group + o, groups), at],
                    block_got.at[o - 1, at],
                    (send5.at[h, o - 1], recv5.at[h, o - 1]),
                    across(o),
                )
                for o in range(1, groups)
            ]
        )
        for copy in over[h]:
            copy.start()
        if h == 0:
            update(chunks // 2, chunks * 3 // 4)
    update(chunks * 3 // 4, chunks)
    twin = (row, col + 1 - 2 * lax.rem(col, 2))
    pairs = cols // 2

    def carry(h, slot, whose, where):
        ref = every.at[whose, pl.ds(*spans[h])]
        return send(ref, ref, (send6.at[h, slot], recv6.at[h, slot]), where)

    near, far, passed = [], [], []
    for h, (low_row, tall) in enumerate(spans):
        at = pl.ds(low_row, tall)
        for copy in over[h]:
            copy.wait()
        value = block[group, at]
        for o in range(1, groups):
            value = value + block_got[o - 1, at]
        every[col, at] = value
        far.append([carry(h, o - 1, col, beside(2 * o)) for o in range(1, pairs)])
        near.append(carry(h, pairs - 1, col, twin))
        for copy in far[h]:
            copy.start()
        near[h].start()
    for h in range(2):
        for o in range(1, pairs):
            far[h][o - 1].wait()
            copy = carry(h, pairs - 1 + o, lax.rem(col - 2 * o + cols, cols), twin)
            copy.start()
            passed.append(copy)
    for copy in near + passed:
        copy.wait()

    result = None
    for c in range(cols):
        receivers = every[c, events:, :]
        amplitude = jnp.concatenate(
            [every[c, e : e + 1, :] * receivers for e in range(events)], axis=0
        )
        value = dot3(split(amplitude), (basis_high[c], basis_low[c]), (1, 1))
        result = value if result is None else result + value
    scale = 1.0 / float(cols * vec.shape[1]) ** 0.5
    seis_ref[...] = (result * scale).reshape(seis_ref.shape)


def shards(
    rows,
    cols,
    vectors,
    reflectors,
    panel_factor,
    station_rows,
    station_weights,
    event_rows,
    event_weights,
    mode_freq,
    mode_damp,
):
    here, wide = vectors.shape
    width = reflectors.shape[1]
    comps, taps = station_rows.shape
    events = event_rows.shape[0]
    comp = comps // rows
    samples = 1024 // cols
    groups = rows // GROUP
    chunk = min(1024, here)
    chunks = here // chunk

    local = jnp.concatenate([station_rows, event_rows]).reshape(-1) - lax.axis_index("row") * here
    weights = jnp.concatenate([station_weights, event_weights]).reshape(-1)
    weights = jnp.where((local >= 0) & (local < here), weights, 0.0)
    local = jnp.clip(local, 0, here - 1)

    parts = 2 if wide % 256 == 0 else 1
    lanes = wide // parts
    piece = width // GROUP
    tall = comp + events
    dma = pltpu.SemaphoreType.DMA
    out_groups, out_cols = max(groups - 1, 1), max(cols - 1, 1)
    in_vmem = pl.BlockSpec(memory_space=pltpu.VMEM)
    in_smem = pl.BlockSpec(memory_space=pltpu.SMEM)
    in_hbm = pl.BlockSpec(memory_space=pltpu.HBM)
    sizes = (parts, groups, cols, chunk, chunks, taps, comp, events, samples)
    rotated, seismograms = pl.pallas_call(
        functools.partial(panel_kernel, sizes),
        out_shape=(
            pltpu.VMEM((here, wide), F32),
            jax.ShapeDtypeStruct((events, comp, samples), F32),
        ),
        in_specs=[in_smem, in_smem, in_hbm, in_hbm, in_hbm, in_hbm, in_hbm],
        out_specs=(in_vmem, in_vmem),
        scratch_shapes=[
            pltpu.VMEM((here, width), F32),
            pltpu.VMEM((1, wide), F32),
            pltpu.VMEM((1, wide), F32),
            pltpu.VMEM((width, width), F32),
            pltpu.VMEM((8, wide), F32),
            pltpu.VMEM((width, wide), BF16),
            pltpu.VMEM((width, wide), BF16),
            pltpu.VMEM((parts, GROUP, piece, lanes), F32),
            pltpu.VMEM((parts, GROUP - 1, piece, lanes), F32),
            pltpu.VMEM((parts, piece, lanes), F32),
            pltpu.VMEM((parts, out_groups, piece, lanes), F32),
            pltpu.VMEM((width, lanes), F32),
            pltpu.VMEM((parts, GROUP, piece, lanes), F32),
            pltpu.VMEM((comps + events, wide), F32),
            pltpu.VMEM((comps + events, width), F32),
            pltpu.VMEM((GROUP, groups, tall, wide), F32),
            pltpu.VMEM((GROUP - 1, groups, tall, wide), F32),
            pltpu.VMEM((groups, tall, wide), F32),
            pltpu.VMEM((out_groups, tall, wide), F32),
            pltpu.VMEM((cols, tall, wide), F32),
            pltpu.VMEM((cols, 8, wide), F32),
            pltpu.VMEM((cols, samples, wide), BF16),
            pltpu.VMEM((cols, samples, wide), BF16),
            dma((chunks, parts + 1)),
            dma((3,)),
            dma((parts, GROUP - 1)),
            dma((parts, GROUP - 1)),
            dma((parts, out_groups)),
            dma((parts, out_groups)),
            dma((parts, GROUP - 1)),
            dma((parts, GROUP - 1)),
            dma((2, GROUP - 1)),
            dma((2, GROUP - 1)),
            dma((2, out_groups)),
            dma((2, out_groups)),
            dma((2, out_cols)),
            dma((2, out_cols)),
            dma((out_cols,)),
            dma((out_cols,)),
        ],
        compiler_params=pltpu.CompilerParams(
            collective_id=0, has_side_effects=True, vmem_limit_bytes=30 * 2**20
        ),
        cost_estimate=pl.CostEstimate(
            flops=12 * here * width * wide,
            bytes_accessed=4 * here * (wide + width),
            transcendentals=0,
        ),
    )(
        local,
        weights,
        vectors,
        reflectors,
        pltpu.with_memory_space_constraint(panel_factor, pltpu.HBM),
        pltpu.with_memory_space_constraint(mode_freq.reshape(1, wide), pltpu.HBM),
        pltpu.with_memory_space_constraint(mode_damp.reshape(1, wide), pltpu.HBM),
    )
    return (rotated, seismograms)


def solution(mesh):
    placed = (P("row", "col"), P("row", None), P(), P(), P(), P(), P(), P("col"), P("col"))
    return jax.shard_map(
        functools.partial(shards, mesh.shape["row"], mesh.shape["col"]),
        mesh=mesh,
        in_specs=placed,
        out_specs=(P("row", "col"), P(None, "row", "col")),
        check_vma=False,
    )
```

time: 87.1 us -> 68.6 us (0.79)
  Pallas kernels: 81.5 us -> 58.5 us
  local copies, waits for them, and re-layouts: 2.37 us -> 7.59 us
    pallas_call x2 -> x1, Pallas kernels: 81.5 us -> 58.5 us  [shards(): pl.pallas_call(functools.partial(panel_kernel, sizes), out_shape=(pltpu.V...]
    unnamed x5 -> x2, local copies, waits for them, and re-layouts: 1.74 us -> 6.96 us
where the time goes in v2:
time: 68.6 us; the launch traced here: 68.2 us
  Pallas kernels  58.5 us (85%)
  local copies, waits for them, and re-layouts  7.59 us (11%)
  other arithmetic  1.48 us (2%)
    pallas_call x1, Pallas kernels, shards(): pl.pallas_call(functools.partial(panel_kernel, sizes), out_shape=(pltpu.V...  58.5 us
    unnamed x2, local copies, waits for them, and re-layouts  6.96 us

profile of v2, /device:TPU:1, one launch (start us, length us, event | category | flops | bytes accessed | tf_op | source)
XLA Modules:
  0.0 68.2 jit_solution(9456250748604810188)
XLA Ops:
  0.6 0.8 %maximum_select_fusion = f32[520,4]{0,1:T(4,128)S(1)} fusion(f32[8,4]{0,1:T(4,128)} %param.15, f32[512,4]{0,1:T(4,128)} %param.13, s32[8,4]{0,1:T(4,128)} %param.14, s32[512,4]{0,1:T(4,128)} %param.12, s32[]{:T(128)S(6)} %mul.3), kind=kLoop, calls=%fused_computation.1 | loop fusion | flops 14560 | bytes 24964 | tf_op jit(solution)/shard_map/jit(_where)/select_n | solution.py:418
  1.4 0.7 %fusion = s32[520,4]{0,1:T(4,128)S(1)} fusion(s32[8,4]{0,1:T(4,128)} %param.14, s32[512,4]{0,1:T(4,128)} %param.12, s32[]{:T(128)S(6)} %mul.3), kind=kLoop, calls=%fused_computation.2 | loop fusion | flops 6240 | bytes 16644 | tf_op jit(solution)/shard_map/jit(clip)/min | solution.py:419
  2.1 0.1 copy.11
  2.3 0.2 min.12.taps_ref
  2.4 0.1 copy.12
  2.6 0.2 select_n.7.weights_ref
  2.8 58.5 %shard_map.104 = (f32[8192,512]{1,0:T(8,128)S(1)}, f32[8,64,256]{2,1,0:T(8,128)S(1)}) custom-call(s32[2080]{0:T(1024)S(1)} %min.12.taps_ref, f32[2080]{0:T(1024)S(1)} %select_n.7.weights_ref, f32[8192,512]{1,0:T(8,128)} %vec_hbm.1, f32[8192,256]{1,0:T(8,128)} %refl_hbm.1, f32[256,256]{1,0:T(8,128)} %factor_hbm.1, f32[1,512]{1,0:T(1,128)} %bitcast.2, ...), custom_call_target="tpu_custom_call" | custom-call | flops 12884901888 | bytes 25165824 | tf_op jit(solution)/shard_map/pallas_call | solution.py:431
  61.3 6.2 %copy.15 = f32[8192,512]{1,0:T(8,128)} copy(f32[8192,512]{1,0:T(8,128)S(1)} %get-tuple-element.2) | data formatting | bytes 33554432
  67.4 0.8 %copy.16 = f32[8,64,256]{2,1,0:T(8,128)} copy(f32[8,64,256]{2,1,0:T(8,128)S(1)} %get-tuple-element.7) | data formatting | bytes 1048576
